TPU v7x, 32 devices: a whole 2x2x4 slice. The times are simulated.
32 devices in a mesh: groups: 2 (over x), node: 8 (over z, core), local: 2 (over y).
Axes of the slice: x: 2, y: 2, z: 4, core: 2. Of those that a mesh axis runs over, the one named last changes fastest.
Arguments:
- tokens: bfloat16 [128, 3584], P(('groups', 'node', 'local')), parts along dimension 0, may hold values from -6 to 6
- node_ids: int32 [128, 4], P(('groups', 'node', 'local')), parts along dimension 0, may hold values from 0 to 7, all different within a row; in each aligned block of 4 rows (0 to 3, 4 to 7, ...) at most 4 rows name the same one
- expert_order: int32 [128, 4, 3], P(('groups', 'node', 'local')), parts along dimension 0, may hold values from 0 to 2, each once within a row
- gate_weights: bfloat16 [128, 4, 2], P(('groups', 'node', 'local')), parts along dimension 0, may hold values from 0.049804688 to 0.59765625
- expert_gate: bfloat16 [24, 3584, 1024], P('node', None, 'local'), may hold values from -0.09375 to 0.09375
- expert_up: bfloat16 [24, 3584, 1024], P('node', None, 'local'), may hold values from -0.09375 to 0.09375
- expert_down: bfloat16 [24, 1024, 3584], P('node', 'local'), may hold values from -0.1875 to 0.1875
- shared_gate: bfloat16 [3584, 1024], P(None, 'local'), may hold values from -0.09375 to 0.09375
- shared_up: bfloat16 [3584, 1024], P(None, 'local'), may hold values from -0.09375 to 0.09375
- shared_down: bfloat16 [1024, 3584], P('local'), may hold values from -0.1875 to 0.1875
Outputs:
- layer_output: bfloat16 [128, 3584], P(('groups', 'node', 'local')), parts along dimension 0
There are 2 independent parts, one for each index of `groups`. A program takes and returns all parts, laid end to end along the dimension named above; an argument that names none is the same for every part. Nothing has to cross between parts.
Inputs may be any that keep to these rules, and one draw needn't show every extreme that they name: `node_ids`: each row names 4 different nodes. Among the rows of one device no node is named by more than 4 rows, and in every draw some device names some node exactly 4 times. `expert_order`: for each row and each of its nodes, the 3 entries are a permutation of 0 to 2.
All inputs are finite; a program needn't handle non-finite values.
Results may differ from a plain program's by a relative error of at most 0.008.
Values may be sent and summed in bfloat16 or wider, within the bound.
A program may use at most 128 MiB of HBM per device.

v0:
```python
import jax
import jax.numpy as jnp
from jax import lax
from jax.sharding import PartitionSpec as P


def expert_terms(row_block, gate_block, w_gate, w_up, w_down):
    gate_part = jnp.einsum("md,edf->mef", row_block, w_gate, preferred_element_type=jnp.float32)
    up_part = jnp.einsum("md,edf->mef", row_block, w_up, preferred_element_type=jnp.float32)
    hidden = (jax.nn.silu(gate_part) * up_part * gate_block.astype(jnp.float32)[:, :, None]).astype(
        jnp.bfloat16
    )
    return jnp.einsum("mef,efd->md", hidden, w_down, preferred_element_type=jnp.float32)


def per_device(
    tokens,
    node_ids,
    expert_order,
    gate_weights,
    expert_gate,
    expert_up,
    expert_down,
    shared_gate,
    shared_up,
    shared_down,
):
    row_count, feature_width = tokens.shape
    node_total = lax.axis_size("node")
    local_total = lax.axis_size("local")
    node_top = node_ids.shape[1]
    experts_here = expert_gate.shape[0]
    capacity = min(row_count, 2 * row_count * node_top // node_total)
    everyone = lax.all_gather(tokens, "local", axis=0, tiled=True)
    shared_g = jnp.dot(everyone, shared_gate, preferred_element_type=jnp.float32)
    shared_u = jnp.dot(everyone, shared_up, preferred_element_type=jnp.float32)
    shared_hidden = (jax.nn.silu(shared_g) * shared_u).astype(jnp.bfloat16)
    shared_sum = lax.psum_scatter(
        jnp.dot(shared_hidden, shared_down, preferred_element_type=jnp.float32).astype(
            jnp.bfloat16
        ),
        "local",
        scatter_dimension=0,
        tiled=True,
    ).astype(jnp.float32)
    node_range = jnp.arange(node_total, dtype=jnp.int32)
    node_hit = (node_ids[:, :, None] == node_range[None, None, :]).astype(jnp.float32)
    sent_mask = jnp.sum(node_hit, axis=1)
    earlier = jnp.cumsum(sent_mask, axis=0) - sent_mask
    slot_range = jnp.arange(capacity, dtype=jnp.float32)
    placing = sent_mask[:, :, None] * (earlier[:, :, None] == slot_range[None, None, :]).astype(
        jnp.float32
    )
    pick_count = gate_weights.shape[2]
    pick_hit = (
        expert_order[:, :, :pick_count, None]
        == jnp.arange(experts_here, dtype=jnp.int32)[None, None, None, :]
    ).astype(jnp.float32)
    node_gate = jnp.sum(pick_hit * gate_weights.astype(jnp.float32)[:, :, :, None], axis=2)
    gate_to_node = jnp.einsum("rkn,rke->rne", node_hit, node_gate)
    placing_narrow = placing.astype(jnp.bfloat16)
    send_rows = jnp.einsum(
        "rnc,rd->ncd", placing_narrow, tokens, preferred_element_type=jnp.float32
    ).astype(jnp.bfloat16)
    send_gates = jnp.einsum("rnc,rne->nce", placing, gate_to_node).astype(jnp.bfloat16)
    row_copies = jnp.broadcast_to(
        send_rows[:, None], (node_total, local_total, capacity, feature_width)
    ).reshape(node_total * local_total, capacity, feature_width)
    gate_copies = jnp.broadcast_to(
        send_gates[:, None], (node_total, local_total, capacity, experts_here)
    ).reshape(node_total * local_total, capacity, experts_here)
    direct_rows, direct_gates = (
        lax.all_to_all(row_copies, ("node", "local"), split_axis=0, concat_axis=0, tiled=True),
        lax.all_to_all(gate_copies, ("node", "local"), split_axis=0, concat_axis=0, tiled=True),
    )
    arrived_rows = direct_rows.reshape(node_total, local_total, capacity, feature_width)
    arrived_gates = direct_gates.reshape(node_total, local_total, capacity, experts_here)
    flat_rows = arrived_rows.reshape(node_total * local_total * capacity, feature_width)
    flat_gates = arrived_gates.reshape(node_total * local_total * capacity, experts_here)
    partial_terms = expert_terms(flat_rows, flat_gates, expert_gate, expert_up, expert_down)
    partial_narrow = partial_terms.astype(jnp.bfloat16).reshape(
        node_total * local_total, capacity, feature_width
    )
    node_back = lax.all_to_all(
        partial_narrow, ("node", "local"), split_axis=0, concat_axis=0, tiled=True
    )
    node_back = node_back.reshape(node_total, local_total, capacity, feature_width)
    returned = jnp.sum(node_back, axis=1, dtype=jnp.float32).astype(jnp.bfloat16)
    routed = jnp.einsum("rnc,ncd->rd", placing_narrow, returned, preferred_element_type=jnp.float32)
    return (routed + shared_sum).astype(jnp.bfloat16)


def solution(mesh):
    return jax.shard_map(
        per_device,
        mesh=mesh,
        in_specs=(
            P(("groups", "node", "local"), None),
            P(("groups", "node", "local"), None),
            P(("groups", "node", "local"), None, None),
            P(("groups", "node", "local"), None, None),
            P("node", None, "local"),
            P("node", None, "local"),
            P("node", "local", None),
            P(None, "local"),
            P(None, "local"),
            P("local", None),
        ),
        out_specs=P(("groups", "node", "local"), None),
        check_vma=False,
    )
```

profile of v0, /device:TPU:0, one launch (start us, length us, event | category | flops | bytes accessed | tf_op | source)
XLA Modules:
  0.0 81.2 jit_solution(11259606040043416435)
XLA Ops:
  0.0 0.8 convert_reduce_fusion
  0.8 0.1 copy.38
  0.9 0.7 copy.36
  1.6 0.7 slice.3
  2.3 0.9 %fusion.20 = bf16[4,8,3]{1,2,0:T(4,128)(2,1)S(1)} fusion(bf16[4,4,3]{1,0,2:T(4,128)(2,1)S(1)} %select_reduce_fusion, s32[4,4]{1,0:T(4,128)} %param.11), kind=kOutput, calls=%fused_computation.30 | convolution fusion | flops 896 | bytes 352 | tf_op jit(solution)/shard_map/rkn,rke->rne/dot_general | solution.py:60
  3.3 0.1 fusion.33
  3.5 0.6 broadcast_in_dim.5
  4.1 7.4 %all-to-all-start.1 = ((bf16[16,4,3]{1,2,0:T(4,128)(2,1)}), bf16[16,4,3]{1,2,0:T(4,128)(2,1)S(1)}, u32[]{:S(2)}, u32[]{:S(2)}) async-start(bf16[16,4,3]{1,2,0:T(4,128)(2,1)} %bitcast.2), calls=%async_computation.1 | async-start | bytes 32768 | tf_op jit(solution)/shard_map/all_to_all | solution.py:74
  11.5 1.0 %convolution_convert_fusion = bf16[8,4,3584]{2,0,1:T(8,128)(2,1)S(1)} fusion(bf16[4,3584]{1,0:T(4,128)(2,1)} %param.10, f32[4,8]{1,0:T(4,128)S(1)} %convert_reduce_fusion, f32[4,8]{1,0:T(4,128)S(1)} %sub.7), kind=kOutput, calls=%fused_computation.2 | convolution fusion | flops 1032448 | bytes 258304 | tf_op jit(solution)/shard_map/rnc,rd->ncd/dot_general | solution.py:62
  12.6 5.3 %all-to-all-done.1 = bf16[16,4,3]{1,2,0:T(4,128)(2,1)S(1)} async-done(((bf16[16,4,3]{1,2,0:T(4,128)(2,1)}), bf16[16,4,3]{1,2,0:T(4,128)(2,1)S(1)}, u32[]{:S(2)}, u32[]{:S(2)}) %all-to-all-start.1) | async-done | bytes 416 | tf_op jit(solution)/shard_map/all_to_all | solution.py:74
  17.9 0.9 %broadcast_in_dim.4 = bf16[8,2,4,3584]{3,2,1,0:T(4,128)(2,1)} broadcast(bf16[8,4,3584]{2,1,0:T(4,128)(2,1)S(1)} %copy.35), dimensions={0,2,3} | broadcast | bytes 688128 | tf_op jit(solution)/shard_map/broadcast_in_dim | solution.py:66
  18.8 3.6 %all-to-all-start = ((bf16[16,4,3584]{2,1,0:T(4,128)(2,1)}), bf16[16,4,3584]{2,1,0:T(4,128)(2,1)S(1)}, u32[]{:S(2)}, u32[]{:S(2)}) async-start(bf16[16,4,3584]{2,1,0:T(4,128)(2,1)} %bitcast.1), calls=%async_computation | async-start | bytes 917504 | tf_op jit(solution)/shard_map/all_to_all | solution.py:73
  22.7 13.0 %all-to-all-done = bf16[16,4,3584]{2,1,0:T(4,128)(2,1)S(1)} async-done(((bf16[16,4,3584]{2,1,0:T(4,128)(2,1)}), bf16[16,4,3584]{2,1,0:T(4,128)(2,1)S(1)}, u32[]{:S(2)}, u32[]{:S(2)}) %all-to-all-start) | async-done | bytes 458784 | tf_op jit(solution)/shard_map/all_to_all | solution.py:73
  35.8 6.1 %fusion.31 = f32[64,3,512]{2,0,1:T(8,128)S(1)} fusion(bf16[64,3584,1]{1,0,2:T(8,128)(2,1)S(1)} %reshape.42, bf16[3,3584,512]{2,1,0:T(8,128)(2,1)} %param.14), kind=kOutput, calls=%fused_computation.42 | convolution fusion | flops 704643072 | bytes 11862016 | tf_op jit(solution)/shard_map/md,edf->mef/dot_general | solution.py:8
  42.0 11.2 %fusion = bf16[64,3584]{1,0:T(8,128)(2,1)S(1)} fusion(bf16[3,512,3584]{2,1,0:T(8,128)(2,1)} %param.16, bf16[64,3584,1]{1,0,2:T(8,128)(2,1)S(1)} %reshape.42, bf16[3,3584,512]{2,1,0:T(8,128)(2,1)} %param.15, f32[64,3,512]{2,0,1:T(8,128)S(1)} %fusion.31, f32[64,3]{0,1:T(4,128)S(1)} %reshape.38), kind=kOutput, calls=%fused_computation.1 | convolution fusion | flops 1410203648 | bytes 23331584 | tf_op jit(solution)/shard_map/mef,efd->md/dot_general | solution.py:13
  53.2 0.9 %reshape.36 = bf16[16,4,3584]{2,1,0:T(4,128)(2,1)} reshape(bf16[64,3584]{1,0:T(8,128)(2,1)S(1)} %fusion) | data formatting | bytes 917504 | tf_op jit(solution)/shard_map/reshape | solution.py:81
  54.1 3.9 %all-to-all-start.2 = ((bf16[16,4,3584]{2,1,0:T(4,128)(2,1)}), bf16[16,4,3584]{2,1,0:T(4,128)(2,1)S(1)}, u32[]{:S(2)}, u32[]{:S(2)}) async-start(bf16[16,4,3584]{2,1,0:T(4,128)(2,1)} %reshape.36), calls=%async_computation.2 | async-start | bytes 917504 | tf_op jit(solution)/shard_map/all_to_all | solution.py:84
  58.0 5.1 %all-gather = bf16[2,4,3584]{2,1,0:T(4,128)(2,1)S(1)} all-gather(bf16[1,4,3584]{2,1,0:T(4,128)(2,1)S(1)} %bitcast.33), channel_id=1, replica_groups=mesh['groups'=2,'node'=8,'local'=2] {'local'}, dimensions={0}, use_global_device_ids=true | all-gather | bytes 86016 | tf_op jit(solution)/shard_map/all_gather | solution.py:34
  63.1 0.6 dynamic-slice
  64.4 2.6 %fusion.32 = f32[8,512]{1,0:T(8,128)S(1)} fusion(bf16[8,3584]{1,0:T(8,128)(2,1)S(1)} %reshape.40, bf16[3584,512]{1,0:T(8,128)(2,1)} %param.17), kind=kOutput, calls=%fused_computation.43 | convolution fusion | flops 29360128 | bytes 3743744 | tf_op jit(solution)/shard_map/dot_general | solution.py:35
  67.0 4.3 %convolution_convert_fusion.1 = bf16[8,3584]{1,0:T(8,128)(2,1)S(1)} fusion(bf16[512,3584]{1,0:T(8,128)(2,1)} %param.19, bf16[8,3584]{1,0:T(8,128)(2,1)S(1)} %reshape.40, bf16[3584,512]{1,0:T(8,128)(2,1)} %param.18, f32[8,512]{1,0:T(8,128)S(1)} %fusion.32), kind=kOutput, calls=%fused_computation.3 | convolution fusion | flops 58773504 | bytes 7471104 | tf_op jit(solution)/shard_map/dot_general | solution.py:39
  71.3 8.8 %all-reduce = bf16[8,3584]{1,0:T(8,128)(2,1)S(1)} all-reduce(bf16[8,3584]{1,0:T(8,128)(2,1)S(1)} %convolution_convert_fusion.1), channel_id=2, replica_groups=mesh['groups'=2,'node'=8,'local'=2] {'local'}, use_global_device_ids=true, to_apply=%region_4.5.clone | all-reduce | flops 28672 | bytes 114688
  80.0 0.3 bitcast_reduce_fusion
  80.3 0.8 %fusion.2 = bf16[4,3584]{1,0:T(4,128)(2,1)} fusion(bf16[8,4,3584]{2,1,0:T(4,128)(2,1)S(1)} %bitcast_reduce_fusion, bf16[8,3584]{1,0:T(8,128)(2,1)S(1)} %all-reduce, u32[]{:T(128)S(6)} %multiply.1, f32[4,8]{1,0:T(4,128)S(1)} %convert_reduce_fusion, f32[4,8]{1,0:T(4,128)S(1)} %sub.7), kind=kOutput, calls=%fused_computation.6 | convolution fusion | flops 960768 | bytes 286980 | tf_op jit(solution)/shard_map/rnc,ncd->rd/dot_general | solution.py:89
  (16 shorter events, 0.8 us)
Async XLA Ops:
  4.1 13.8 %all-to-all-start.1 = ((bf16[16,4,3]{1,2,0:T(4,128)(2,1)}), bf16[16,4,3]{1,2,0:T(4,128)(2,1)S(1)}, u32[]{:S(2)}, u32[]{:S(2)}) async-start(bf16[16,4,3]{1,2,0:T(4,128)(2,1)} %bitcast.2), calls=%async_computation.1 | async-start | bytes 32768 | tf_op jit(solution)/shard_map/all_to_all | solution.py:74
  18.8 16.9 %all-to-all-start = ((bf16[16,4,3584]{2,1,0:T(4,128)(2,1)}), bf16[16,4,3584]{2,1,0:T(4,128)(2,1)S(1)}, u32[]{:S(2)}, u32[]{:S(2)}) async-start(bf16[16,4,3584]{2,1,0:T(4,128)(2,1)} %bitcast.1), calls=%async_computation | async-start | bytes 917504 | tf_op jit(solution)/shard_map/all_to_all | solution.py:73
  41.9 16.0 %copy-start = (bf16[4,3584]{1,0:T(4,128)(2,1)S(1)}, bf16[4,3584]{1,0:T(4,128)(2,1)}, u32[]{:S(2)}) copy-start(bf16[4,3584]{1,0:T(4,128)(2,1)} %param.10) | copy-start | bytes 86020
  42.0 21.2 %copy-start.1 = (u32[32]{0:T(128)S(1)}, u32[32]{0:T(128)}, u32[]{:S(2)}) copy-start(u32[32]{0:T(128)} %constant.23) | copy-start | bytes 388
  54.1 25.9 %all-to-all-start.2 = ((bf16[16,4,3584]{2,1,0:T(4,128)(2,1)}), bf16[16,4,3584]{2,1,0:T(4,128)(2,1)S(1)}, u32[]{:S(2)}, u32[]{:S(2)}) async-start(bf16[16,4,3584]{2,1,0:T(4,128)(2,1)} %reshape.36), calls=%async_computation.2 | async-start | bytes 917504 | tf_op jit(solution)/shard_map/all_to_all | solution.py:84
where the time goes:
time: 81.8 us; the launch traced here: 81.2 us
  matrix products  27.1 us (33%)
  waiting for transfers between devices  18.3 us (22%)
  starting transfers between devices  14.8 us (18%)
  blocking collectives  13.9 us (17%)
  local copies, waits for them, and re-layouts  5.16 us (6%)
  other arithmetic  1.12 us (1%)
    all_to_all x1, waiting for transfers between devices, per_device(): lax.all_to_all(row_copies, ('node', 'local'), split_axis=0, concat_axis=0...  13 us
    dot_general x1, matrix products, expert_terms(): jnp.einsum('mef,efd->md', hidden, w_down, preferred_element_type=jnp.floa...  11.2 us
    unnamed x1, blocking collectives  8.77 us
    all_to_all x1, starting transfers between devices, per_device(): lax.all_to_all(gate_copies, ('node', 'local'), split_axis=0, concat_axis=...  7.39 us
    dot_general x1, matrix products, expert_terms(): jnp.einsum('md,edf->mef', row_block, w_gate, preferred_element_type=jnp.f...  6.13 us
    all_to_all x1, waiting for transfers between devices, per_device(): lax.all_to_all(gate_copies, ('node', 'local'), split_axis=0, concat_axis=...  5.3 us
    all_gather x1, blocking collectives, per_device(): everyone = lax.all_gather(tokens, 'local', axis=0, tiled=True)  5.09 us
    dot_general x1, matrix products, per_device(): jnp.dot(shared_hidden, shared_down, preferred_element_type=jnp.float32)  4.3 us
  transfers between devices with their start and end apart: 3, of which 2 were waited for; matrix products, arithmetic and copies ran while one was open for 11% of the time, Pallas kernels for 0%

commit v1 on v0

v1 whole, which is shorter than its diff:
```python
import functools

import jax
import jax.numpy as jnp
from jax import lax
from jax.experimental import pallas as pl
from jax.experimental.pallas import tpu as pltpu
from jax.sharding import PartitionSpec as P

MESH = pl.DeviceIdType.MESH
LANES = 128
CHUNKS = 4


def layer_kernel(
    nodes,
    locals_,
    packed,
    w_gate,
    w_up,
    w_down,
    s_gate,
    s_up,
    s_down,
    out,
    gate_v,
    up_v,
    sgate_v,
    sup_v,
    down_v,
    gathered,
    rows_wide,
    rows,
    hidden,
    sib_out,
    sib_in,
    mine,
    piece_out,
    piece_in,
    gate_sem,
    up_sem,
    sg_sem,
    su_sem,
    down_sem,
    g_send,
    g_recv,
    f_send,
    f_recv,
    s_send,
    s_recv,
    b_send,
    b_recv,
):
    experts, width, units = w_gate.shape
    row_count = packed.shape[0]
    chunks, _, chunk = down_v.shape
    peers = (nodes // 2) * locals_
    node = lax.axis_index("node")
    local = lax.axis_index("local")
    core = lax.rem(node, 2)
    my_peer = (node // 2) * locals_ + local

    def peer_id(peer, parity):
        return {"node": 2 * (peer // locals_) + parity, "local": lax.rem(peer, locals_)}

    def place(peer, parity):
        return (2 * (peer // locals_) + parity) * locals_ + lax.rem(peer, locals_)

    sibling = {"node": node + 1 - 2 * core, "local": local}

    blocks = s_gate.shape[1] // LANES
    share = nodes // blocks
    block_start = pl.multiple_of((node // share) * LANES, LANES)
    loads = []
    for e in range(experts):
        loads.append(pltpu.make_async_copy(w_gate.at[e], gate_v.at[e], gate_sem.at[e]))
        loads.append(pltpu.make_async_copy(w_up.at[e], up_v.at[e], up_sem.at[e]))
    sg_load = pltpu.make_async_copy(s_gate.at[:, pl.ds(block_start, LANES)], sgate_v, sg_sem)
    su_load = pltpu.make_async_copy(s_up.at[:, pl.ds(block_start, LANES)], sup_v, su_sem)
    loads += [sg_load, su_load]
    down_loads = []
    for c in range(chunks):
        cols = pl.ds(c * chunk, chunk)
        group = [
            pltpu.make_async_copy(
                w_down.at[e, :, cols],
                down_v.at[c, pl.ds(e * units, units), :],
                down_sem.at[c, e],
            )
            for e in range(experts)
        ]
        group.append(
            pltpu.make_async_copy(
                s_down.at[pl.ds(block_start, LANES), cols],
                down_v.at[c, pl.ds(experts * units, LANES), :],
                down_sem.at[c, experts],
            )
        )
        down_loads.append(group)
        loads += group
    for load in loads:
        load.start()

    barrier = pltpu.get_barrier_semaphore()
    pl.semaphore_signal(barrier, inc=1, device_id=sibling, device_id_type=MESH)

    def greet(step, carry):
        peer = lax.rem(my_peer + step, peers)
        pl.semaphore_signal(barrier, inc=1, device_id=peer_id(peer, core), device_id_type=MESH)
        return carry

    lax.fori_loop(1, peers, greet, 0)
    pl.semaphore_wait(barrier, peers)

    def gather_copy(step):
        return pltpu.make_async_remote_copy(
            src_ref=packed,
            dst_ref=gathered.at[place(my_peer, core)],
            send_sem=g_send.at[step],
            recv_sem=g_recv.at[step],
            device_id=peer_id(lax.rem(my_peer + step, peers), core),
            device_id_type=MESH,
        )

    def forward_copy(step):
        where = place(lax.rem(my_peer - step + peers, peers), core)
        return pltpu.make_async_remote_copy(
            src_ref=gathered.at[where],
            dst_ref=gathered.at[where],
            send_sem=f_send.at[step],
            recv_sem=f_recv.at[step],
            device_id=sibling,
            device_id_type=MESH,
        )

    own_forward = pltpu.make_async_remote_copy(
        src_ref=packed,
        dst_ref=gathered.at[place(my_peer, core)],
        send_sem=f_send.at[0],
        recv_sem=f_recv.at[0],
        device_id=sibling,
        device_id_type=MESH,
    )

    def start_gather(step, carry):
        gather_copy(step).start()
        return carry

    lax.fori_loop(1, peers, start_gather, 0)
    own_forward.start()
    gathered[place(my_peer, core)] = packed[...]

    def pass_on(step, carry):
        gather_copy(step).wait_recv()
        forward_copy(step).start()
        return carry

    lax.fori_loop(1, peers, pass_on, 0)

    def arrived(step, carry):
        forward_copy(step).wait_recv()
        return carry

    lax.fori_loop(0, peers, arrived, 0)
    for i in range(nodes * locals_):
        rows_wide[i * row_count : (i + 1) * row_count, :] = gathered[i].astype(jnp.float32)
    rows[...] = rows_wide[:, :width].astype(jnp.bfloat16)

    gates = rows_wide[:, width:]
    lane = lax.broadcasted_iota(jnp.int32, gates.shape, 1)

    def expert(e, carry):
        pltpu.make_async_copy(w_gate.at[e], gate_v.at[e], gate_sem.at[e]).wait()
        g = jnp.dot(rows[...], gate_v[e], preferred_element_type=jnp.float32)
        pltpu.make_async_copy(w_up.at[e], up_v.at[e], up_sem.at[e]).wait()
        u = jnp.dot(rows[...], up_v[e], preferred_element_type=jnp.float32)
        weight = jnp.sum(jnp.where(lane == node * experts + e, gates, 0.0), axis=1, keepdims=True)
        value = g / (1.0 + jnp.exp(-g)) * u * weight
        hidden[:, pl.ds(pl.multiple_of(e * units, LANES), units)] = value.astype(jnp.bfloat16)
        return carry

    lax.fori_loop(0, experts, expert, 0)
    sg_load.wait()
    g = jnp.dot(rows[...], sgate_v[...], preferred_element_type=jnp.float32)
    su_load.wait()
    u = jnp.dot(rows[...], sup_v[...], preferred_element_type=jnp.float32)
    part = LANES // share
    first = lax.rem(node, share) * part
    unit = lax.broadcasted_iota(jnp.int32, g.shape, 1)
    owned = jnp.logical_and(unit >= first, unit < first + part)
    value = jnp.where(owned, g / (1.0 + jnp.exp(-g)) * u, 0.0)
    hidden[:, experts * units :] = value.astype(jnp.bfloat16)

    def sib_copy(c):
        return pltpu.make_async_remote_copy(
            src_ref=sib_out.at[c],
            dst_ref=sib_in.at[c],
            send_sem=s_send.at[c],
            recv_sem=s_recv.at[c],
            device_id=sibling,
            device_id_type=MESH,
        )

    def piece_copy(c, step):
        peer = lax.rem(my_peer + step, peers)
        return pltpu.make_async_remote_copy(
            src_ref=piece_out.at[c, peer],
            dst_ref=piece_in.at[c, step],
            send_sem=b_send.at[c, step],
            recv_sem=b_recv.at[c, step],
            device_id=peer_id(peer, core),
            device_id_type=MESH,
        )

    span = locals_ * row_count

    def project(c):
        for load in down_loads[c]:
            load.wait()
        total = jnp.dot(hidden[...], down_v[c], preferred_element_type=jnp.float32)
        for z in range(nodes // 2):
            even = total[2 * z * span : (2 * z + 1) * span]
            odd = total[(2 * z + 1) * span : (2 * z + 2) * span]
            mine[c, z * span : (z + 1) * span, :] = jnp.where(core == 0, even, odd)
            sib_out[c, z * span : (z + 1) * span, :] = jnp.where(core == 0, odd, even).astype(
                jnp.bfloat16
            )
        sib_copy(c).start()

    def send_on(c):
        sib_copy(c).wait_recv()
        both = (mine[c] + sib_in[c].astype(jnp.float32)).astype(jnp.bfloat16)
        for peer in range(peers):
            piece_out[c, peer] = both[peer * row_count : (peer + 1) * row_count]

        def start_piece(step, carry):
            piece_copy(c, step).start()
            return carry

        lax.fori_loop(1, peers, start_piece, 0)

    def finish(c):
        def add(step, total):
            piece_copy(c, step).wait_recv()
            return total + piece_in[c, step].astype(jnp.float32)

        total = lax.fori_loop(1, peers, add, piece_out[c, my_peer].astype(jnp.float32))
        out[:, c * chunk : (c + 1) * chunk] = total.astype(jnp.bfloat16)

    for c in range(chunks):
        project(c)
        if c >= 1:
            send_on(c - 1)
    send_on(chunks - 1)
    for c in range(chunks):
        finish(c)

    own_forward.wait_send()

    def sent(step, carry):
        gather_copy(step).wait_send()
        forward_copy(step).wait_send()
        for c in range(chunks):
            piece_copy(c, step).wait_send()
        return carry

    lax.fori_loop(1, peers, sent, 0)
    for c in range(chunks):
        sib_copy(c).wait_send()


def per_device(
    nodes,
    locals_,
    tokens,
    node_ids,
    expert_order,
    gate_weights,
    expert_gate,
    expert_up,
    expert_down,
    shared_gate,
    shared_up,
    shared_down,
):
    row_count, width = tokens.shape
    experts, _, units = expert_gate.shape
    pick = gate_weights.shape[2]
    gate_lanes = -(-nodes * experts // LANES) * LANES
    target = node_ids[:, :, None] * experts + expert_order[:, :, :pick]
    hit = target[:, :, :, None] == jnp.arange(gate_lanes, dtype=jnp.int32)
    gates = jnp.sum(
        jnp.where(hit, gate_weights.astype(jnp.float32)[:, :, :, None], 0.0), axis=(1, 2)
    ).astype(jnp.bfloat16)
    packed = jnp.concatenate([tokens, gates], axis=1)
    full = width + gate_lanes
    devices = nodes * locals_
    peers = devices // 2
    total = devices * row_count
    chunk = width // CHUNKS
    deep = experts * units + LANES
    half = total // 2
    bf, f32 = jnp.bfloat16, jnp.float32
    dma = pltpu.SemaphoreType.DMA
    hbm = pl.BlockSpec(memory_space=pl.ANY)
    vmem = pl.BlockSpec(memory_space=pltpu.VMEM)
    return pl.pallas_call(
        functools.partial(layer_kernel, nodes, locals_),
        out_shape=jax.ShapeDtypeStruct((row_count, width), bf),
        in_specs=[vmem] + [hbm] * 6,
        out_specs=vmem,
        scratch_shapes=[
            pltpu.VMEM((experts, width, units), bf),
            pltpu.VMEM((experts, width, units), bf),
            pltpu.VMEM((width, LANES), bf),
            pltpu.VMEM((width, LANES), bf),
            pltpu.VMEM((CHUNKS, deep, chunk), bf),
            pltpu.VMEM((devices, row_count, full), bf),
            pltpu.VMEM((total, full), f32),
            pltpu.VMEM((total, width), bf),
            pltpu.VMEM((total, deep), bf),
            pltpu.VMEM((CHUNKS, half, chunk), bf),
            pltpu.VMEM((CHUNKS, half, chunk), bf),
            pltpu.VMEM((CHUNKS, half, chunk), f32),
            pltpu.VMEM((CHUNKS, peers, row_count, chunk), bf),
            pltpu.VMEM((CHUNKS, peers, row_count, chunk), bf),
            dma((experts,)),
            dma((experts,)),
            dma,
            dma,
            dma((CHUNKS, experts + 1)),
            dma((peers,)),
            dma((peers,)),
            dma((peers,)),
            dma((peers,)),
            dma((CHUNKS,)),
            dma((CHUNKS,)),
            dma((CHUNKS, peers)),
            dma((CHUNKS, peers)),
        ],
        compiler_params=pltpu.CompilerParams(
            collective_id=0, has_side_effects=True, vmem_limit_bytes=60 * 2**20
        ),
        cost_estimate=pl.CostEstimate(
            flops=6 * total * width * deep,
            bytes_accessed=6 * width * deep,
            transcendentals=total * deep,
        ),
    )(packed, expert_gate, expert_up, expert_down, shared_gate, shared_up, shared_down)


def solution(mesh):
    return jax.shard_map(
        functools.partial(per_device, mesh.shape["node"], mesh.shape["local"]),
        mesh=mesh,
        in_specs=(
            P(("groups", "node", "local"), None),
            P(("groups", "node", "local"), None),
            P(("groups", "node", "local"), None, None),
            P(("groups", "node", "local"), None, None),
            P("node", None, "local"),
            P("node", None, "local"),
            P("node", "local", None),
            P(None, "local"),
            P(None, "local"),
            P("local", None),
        ),
        out_specs=P(("groups", "node", "local"), None),
        check_vma=False,
    )
```

time: 81.8 us -> 35.4 us (0.43)
  Pallas kernels: 0 us -> 30.1 us
  matrix products: 27.1 us -> 0 us
  waiting for transfers between devices: 18.3 us -> 0 us
  starting transfers between devices: 14.8 us -> 0 us
  blocking collectives: 13.9 us -> 0 us
  local copies, waits for them, and re-layouts: 5.16 us -> 1.37 us
  other arithmetic: 1.12 us -> 3.52 us
    pallas_call x0 -> x1, Pallas kernels: none -> 30.1 us  [per_device(): pl.pallas_call(functools.partial(layer_kernel, nodes, locals_), out_shape...]
    dot_general x8 -> x0, matrix products: 27.1 us -> none  [the longest x1 11.2 us: expert_terms(): jnp.einsum('mef,efd->md', hidden, w_down, preferred_element_type=jnp.floa...]
    all_to_all x3 -> x0, waiting for transfers between devices: 18.3 us -> none  [the longest x1 13 us: per_device(): lax.all_to_all(row_copies, ('node', 'local'), split_axis=0, concat_axis=0...]
    all_to_all x3 -> x0, starting transfers between devices: 14.8 us -> none  [the longest x1 7.39 us: per_device(): lax.all_to_all(gate_copies, ('node', 'local'), split_axis=0, concat_axis=...]
    unnamed x1 -> x0, blocking collectives: 8.77 us -> none
    all_gather x1 -> x0, blocking collectives: 5.09 us -> none  [per_device(): everyone = lax.all_gather(tokens, 'local', axis=0, tiled=True)]
    broadcast_in_dim x2 -> x0, local copies, waits for them, and re-layouts: 1.51 us -> none  [the longest x1 0.89 us: per_device(): jnp.broadcast_to(send_rows[:, None], (node_total, local_total, capacity,...]
    concatenate x0 -> x1, other arithmetic: none -> 1.37 us  [per_device(): packed = jnp.concatenate([tokens, gates], axis=1)]
  transfers between devices with their start and end apart: 3 -> 0, of which waited for: 2 -> 0; matrix products, arithmetic and copies ran while one was open for 11% -> 0% of each run, Pallas kernels for 0% -> 0%
where the time goes in v1:
time: 35.4 us; the launch traced here: 35 us
  Pallas kernels  30.1 us (85%)
  other arithmetic  3.52 us (10%)
  local copies, waits for them, and re-layouts  1.37 us (4%)
    pallas_call x1, Pallas kernels, per_device(): pl.pallas_call(functools.partial(layer_kernel, nodes, locals_), out_shape...  30.1 us
    unnamed x1, local copies, waits for them, and re-layouts  1.37 us
    concatenate x1, other arithmetic, per_device(): packed = jnp.concatenate([tokens, gates], axis=1)  1.37 us

profile of v1, /device:TPU:0, one launch (start us, length us, event | category | flops | bytes accessed | tf_op | source)
XLA Modules:
  0.0 35.0 jit_solution(3123219571891390790)
XLA Ops:
  0.0 0.7 %broadcast_multiply_fusion = s32[4,4]{1,0:T(4,128)S(1)} fusion(s32[4,4]{1,0:T(4,128)} %param.11), kind=kLoop, calls=%fused_computation.4 | loop fusion | flops 16 | bytes 128 | tf_op jit(solution)/shard_map/mul | solution.py:290
  0.7 0.7 %slice_add_fusion = s32[4,4,2]{1,0,2:T(4,128)S(1)} fusion(s32[4,4,3]{1,0,2:T(4,128)} %param.12, s32[4,4]{1,0:T(4,128)S(1)} %broadcast_multiply_fusion), kind=kLoop, calls=%fused_computation.3 | loop fusion | flops 32 | bytes 320 | tf_op jit(solution)/shard_map/add | solution.py:290
  1.4 0.7 %convert_element_type.6 = f32[4,4,2]{1,2,0:T(2,128)S(1)} convert(bf16[4,4,2]{1,2,0:T(2,128)(2,1)} %param.13) | non-fusion elementwise | flops 32 | bytes 192 | tf_op jit(solution)/shard_map/convert_element_type | solution.py:293
  2.1 0.1 select_reduce_fusion
  2.2 1.4 %pad_maximum_fusion.packed = bf16[4,3712]{1,0:T(4,128)(2,1)} fusion(bf16[4,128]{1,0:T(4,128)(2,1)S(1)} %select_reduce_fusion, bf16[4,3584]{1,0:T(4,128)(2,1)} %param.10), kind=kLoop, calls=%fused_computation | loop fusion | flops 59392 | bytes 59392 | tf_op jit(solution)/shard_map/concatenate | solution.py:295
  3.5 30.1 %shard_map.100 = bf16[4,3584]{1,0:T(4,128)(2,1)} custom-call(bf16[4,3712]{1,0:T(4,128)(2,1)} %pad_maximum_fusion.packed, bf16[3,3584,512]{2,1,0:T(8,128)(2,1)} %w_gate.1, bf16[3,3584,512]{2,1,0:T(8,128)(2,1)} %w_up.1, bf16[3,512,3584]{2,1,0:T(8,128)(2,1)} %w_down.1, bf16[3584,512]{1,0:T(8,128)(2,1)} %s_gate.1, bf16[3584,512]{1,0:T(8,128)(2,1)} %s_up.1, ...), custom_call_target="tpu_custom_call" | custom-call | flops 2290089984 | bytes 35782656 | tf_op jit(solution)/shard_map/pallas_call | solution.py:307
  33.7 1.4 %copy.15 = bf16[4,3584]{1,0:T(4,128)(2,1)} copy(bf16[4,3584]{1,0:T(4,128)(2,1)} %shard_map.100) | data formatting | bytes 57344
  (1 shorter events, 0.0 us)

commit v2 on v1

--- a/solution.py
+++ b/solution.py
@@ -15,7 +15,10 @@
 def layer_kernel(
     nodes,
     locals_,
-    packed,
+    tokens,
+    node_ids,
+    expert_order,
+    gate_weights,
     w_gate,
     w_up,
     w_down,
@@ -28,6 +31,7 @@
     sgate_v,
     sup_v,
     down_v,
+    packed,
     gathered,
     rows_wide,
     rows,
@@ -52,7 +56,8 @@
     b_recv,
 ):
     experts, width, units = w_gate.shape
-    row_count = packed.shape[0]
+    row_count, top = node_ids.shape
+    pick = gate_weights.shape[1]
     chunks, _, chunk = down_v.shape
     peers = (nodes // 2) * locals_
     node = lax.axis_index("node")
@@ -110,6 +115,22 @@
         return carry
 
     lax.fori_loop(1, peers, greet, 0)
+
+    packed[:, :width] = tokens[...]
+    lanes = packed.shape[1] - width
+    lane = lax.broadcasted_iota(jnp.int32, (row_count, lanes), 1)
+    row_at = lax.broadcasted_iota(jnp.int32, (row_count, top), 0)
+    own_gates = jnp.zeros((row_count, lanes), jnp.float32)
+    for p in range(pick):
+        key = node_ids[...] * experts + expert_order[p]
+        weights = jnp.zeros((row_count, top), jnp.float32)
+        for t in range(row_count):
+            weights = jnp.where(row_at == t, gate_weights[t].astype(jnp.float32)[p : p + 1], weights)
+        for k in range(top):
+            own_gates = own_gates + jnp.where(
+                lane == key[:, k : k + 1], weights[:, k : k + 1], 0.0
+            )
+    packed[:, width:] = own_gates.astype(jnp.bfloat16)
     pl.semaphore_wait(barrier, peers)
 
     def gather_copy(step):
@@ -245,7 +266,7 @@
             return total + piece_in[c, step].astype(jnp.float32)
 
         total = lax.fori_loop(1, peers, add, piece_out[c, my_peer].astype(jnp.float32))
-        out[:, c * chunk : (c + 1) * chunk] = total.astype(jnp.bfloat16)
+        out[:, c * chunk : (c + 1) * chunk] = total.astype(out.dtype)
 
     for c in range(chunks):
         project(c)
@@ -285,14 +306,9 @@
 ):
     row_count, width = tokens.shape
     experts, _, units = expert_gate.shape
-    pick = gate_weights.shape[2]
     gate_lanes = -(-nodes * experts // LANES) * LANES
-    target = node_ids[:, :, None] * experts + expert_order[:, :, :pick]
-    hit = target[:, :, :, None] == jnp.arange(gate_lanes, dtype=jnp.int32)
-    gates = jnp.sum(
-        jnp.where(hit, gate_weights.astype(jnp.float32)[:, :, :, None], 0.0), axis=(1, 2)
-    ).astype(jnp.bfloat16)
-    packed = jnp.concatenate([tokens, gates], axis=1)
+    order = jnp.transpose(expert_order, (2, 0, 1))
+    weights = jnp.transpose(gate_weights, (0, 2, 1))
     full = width + gate_lanes
     devices = nodes * locals_
     peers = devices // 2
@@ -304,10 +320,10 @@
     dma = pltpu.SemaphoreType.DMA
     hbm = pl.BlockSpec(memory_space=pl.ANY)
     vmem = pl.BlockSpec(memory_space=pltpu.VMEM)
-    return pl.pallas_call(
+    result = pl.pallas_call(
         functools.partial(layer_kernel, nodes, locals_),
-        out_shape=jax.ShapeDtypeStruct((row_count, width), bf),
-        in_specs=[vmem] + [hbm] * 6,
+        out_shape=jax.ShapeDtypeStruct((row_count, width), f32),
+        in_specs=[vmem] * 4 + [hbm] * 6,
         out_specs=vmem,
         scratch_shapes=[
             pltpu.VMEM((experts, width, units), bf),
@@ -315,6 +331,7 @@
             pltpu.VMEM((width, LANES), bf),
             pltpu.VMEM((width, LANES), bf),
             pltpu.VMEM((CHUNKS, deep, chunk), bf),
+            pltpu.VMEM((row_count, full), bf),
             pltpu.VMEM((devices, row_count, full), bf),
             pltpu.VMEM((total, full), f32),
             pltpu.VMEM((total, width), bf),
@@ -346,7 +363,19 @@
             bytes_accessed=6 * width * deep,
             transcendentals=total * deep,
         ),
-    )(packed, expert_gate, expert_up, expert_down, shared_gate, shared_up, shared_down)
+    )(
+        tokens,
+        node_ids,
+        order,
+        weights,
+        expert_gate,
+        expert_up,
+        expert_down,
+        shared_gate,
+        shared_up,
+        shared_down,
+    )
+    return result.astype(bf)
 
 
 def solution(mesh):

time: 35.4 us -> 31.8 us (0.90)
  other arithmetic: 3.52 us -> 1.44 us
  local copies, waits for them, and re-layouts: 1.37 us -> 0 us
    unnamed x1 -> x0, local copies, waits for them, and re-layouts: 1.37 us -> none
    concatenate x1 -> x0, other arithmetic: 1.37 us -> none  [per_device(): packed = jnp.concatenate([tokens, gates], axis=1)]
    convert_element_type x1, other arithmetic: 0.68 us -> 1.44 us  [per_device(): return result.astype(bf)]
    add x1 -> x0, other arithmetic: 0.69 us -> none  [per_device(): target = node_ids[:, :, None] * experts + expert_order[:, :, :pick]]
    mul x1 -> x0, other arithmetic: 0.68 us -> none  [per_device(): target = node_ids[:, :, None] * experts + expert_order[:, :, :pick]]
where the time goes in v2:
time: 31.8 us; the launch traced here: 31.6 us
  Pallas kernels  30.2 us (95%)
  other arithmetic  1.44 us (5%)
    pallas_call x1, Pallas kernels, per_device(): pl.pallas_call(functools.partial(layer_kernel, nodes, locals_), out_shape...  30.2 us
    convert_element_type x1, other arithmetic, per_device(): return result.astype(bf)  1.44 us

profile of v2, /device:TPU:0, one launch (start us, length us, event | category | flops | bytes accessed | tf_op | source)
XLA Modules:
  0.0 31.6 jit_solution(15310915111349118999)
XLA Ops:
  0.0 30.2 %shard_map.100 = f32[4,3584]{1,0:T(4,128)} custom-call(bf16[4,3584]{1,0:T(4,128)(2,1)} %tokens.1, s32[4,4]{1,0:T(4,128)} %node_ids.1, s32[3,4,4]{2,1,0:T(4,128)} %bitcast.2, bf16[4,2,4]{2,1,0:T(2,128)(2,1)} %bitcast.3, bf16[3,3584,512]{2,1,0:T(8,128)(2,1)} %w_gate.1, bf16[3,3584,512]{2,1,0:T(8,128)(2,1)} %w_up.1, bf16[3,512,3584]{2,1,0:T(8,128)(2,1)} %w_down.1, ...), custom_call_target="tpu_custom_call" | custom-call | flops 2290089984 | bytes 35782656 | tf_op jit(solution)/shard_map/pallas_call | solution.py:323
  30.2 1.4 %convert_element_type.3 = bf16[4,3584]{1,0:T(4,128)(2,1)} convert(f32[4,3584]{1,0:T(4,128)} %shard_map.100) | non-fusion elementwise | flops 14336 | bytes 86016 | tf_op jit(solution)/shard_map/convert_element_type | solution.py:378
